TPU v7x, 32 devices: a whole 2x2x4 slice. The times are simulated.
32 devices in a mesh: seq: 8 (over z, y), res: 4 (over x, core).
Axes of the slice: x: 2, y: 2, z: 4, core: 2. Of those that a mesh axis runs over, the one named last changes fastest.
Arguments:
- homolog_profile: bfloat16 [64, 512, 256], P('seq', 'res'), may hold values from -6 to 6
- couplings_tensor: bfloat16 [512, 512, 128], P('res', 'seq'), may hold values from -6 to 6
- present_entries: int32 [64, 512], P('seq', 'res'), may hold values 0 or 1
- resolved_positions: int32 [512], P('res'), may hold values 0 or 1
- coupling_logit_matrix: bfloat16 [128, 8], replicated
- horizontal_asking_matrix: bfloat16 [256, 256], replicated
- horizontal_lookup_matrix: bfloat16 [256, 256], replicated, may hold values from -0.375 to 0.375
- horizontal_content_matrix: bfloat16 [256, 256], replicated, may hold values from -0.375 to 0.375
- horizontal_sigmoid_matrix: bfloat16 [256, 256], replicated, may hold values from -0.375 to 0.375
- horizontal_final_matrix: bfloat16 [256, 256], replicated, may hold values from -0.375 to 0.375
- vertical_asking_matrix: bfloat16 [256, 256], replicated
- vertical_lookup_matrix: bfloat16 [256, 256], replicated, may hold values from -0.375 to 0.375
- vertical_content_matrix: bfloat16 [256, 256], replicated, may hold values from -0.375 to 0.375
- vertical_sigmoid_matrix: bfloat16 [256, 256], replicated, may hold values from -0.375 to 0.375
- vertical_final_matrix: bfloat16 [256, 256], replicated, may hold values from -0.375 to 0.375
- widening_matrix: bfloat16 [256, 1024], replicated, may hold values from -0.375 to 0.375
- narrowing_matrix: bfloat16 [1024, 256], replicated, may hold values from -0.1875 to 0.1875
Outputs:
- msa_next: bfloat16 [64, 512, 256], P('seq', 'res')
All inputs are finite; a program needn't handle non-finite values. No bound on the sum of `present_entries` or of `resolved_positions` on one device may be relied on, other than what follows from the above.
Results may differ from a plain program's by a relative error of at most 0.014.
The roundings to bfloat16 on the way count: a program that leaves them out, or rounds other values in their place, can miss the bound.
Values may be sent and summed in bfloat16 or wider, within the bound.
A program may use at most 128 MiB of HBM per device.

v0:
```python
import math

import jax
import jax.numpy as jnp
from jax import lax
from jax.sharding import PartitionSpec as P

HEADS = 8
HEAD_DIM = 32


EPS = 1e-05
MASK_SCALE = 1000000000.0


def standardize_features_fn(values):
    values = values.astype(jnp.float32)
    center = values - jnp.mean(values, -1, keepdims=True)
    spread = jnp.mean(center * center, -1, keepdims=True)
    return center * lax.rsqrt(spread + EPS)


def on_device(
    homolog_profile,
    couplings_tensor,
    present_entries,
    resolved_positions,
    coupling_logit_matrix,
    horizontal_asking_matrix,
    horizontal_lookup_matrix,
    horizontal_content_matrix,
    horizontal_sigmoid_matrix,
    horizontal_final_matrix,
    vertical_asking_matrix,
    vertical_lookup_matrix,
    vertical_content_matrix,
    vertical_sigmoid_matrix,
    vertical_final_matrix,
    widening_matrix,
    narrowing_matrix,
):
    number_entries, homolog_groups, embedding_depth = homolog_profile.shape
    head_dim = embedding_depth // HEADS
    scale = HEAD_DIM ** (-0.5)
    bias = jnp.einsum(
        "ijc,ch->hij",
        standardize_features_fn(couplings_tensor),
        coupling_logit_matrix.astype(jnp.float32),
        precision=lax.Precision.HIGHEST,
    ).astype(jnp.bfloat16)
    bias_all = lax.all_gather(bias, "seq", axis=2, tiled=True)
    lone_source_tensor = standardize_features_fn(homolog_profile).astype(jnp.bfloat16)
    query = (
        jnp.dot(lone_source_tensor, horizontal_asking_matrix, preferred_element_type=jnp.float32)
        * scale
    ).astype(jnp.bfloat16)
    query = query.reshape(number_entries, homolog_groups, HEADS, head_dim)
    gate = jax.nn.sigmoid(
        jnp.dot(lone_source_tensor, horizontal_sigmoid_matrix, preferred_element_type=jnp.float32)
    )
    key_valid = (present_entries * resolved_positions[None, :]).astype(jnp.bfloat16)
    start_state = (
        jnp.full((number_entries, HEADS, homolog_groups), -1e30, jnp.float32),
        jnp.zeros((number_entries, HEADS, homolog_groups), jnp.float32),
        jnp.zeros((number_entries, HEADS, homolog_groups, head_dim), jnp.float32),
    )
    keys = jnp.dot(
        lone_source_tensor, horizontal_lookup_matrix, preferred_element_type=jnp.float32
    ).astype(jnp.bfloat16)
    values = jnp.dot(
        lone_source_tensor, horizontal_content_matrix, preferred_element_type=jnp.float32
    ).astype(jnp.bfloat16)
    pieces = (
        lax.all_gather(keys, "res", axis=1, tiled=True),
        lax.all_gather(values, "res", axis=1, tiled=True),
        lax.all_gather(key_valid, "res", axis=1, tiled=True),
    )
    keys = pieces[0]
    values = pieces[1]
    okay = pieces[2]
    stretch_extent = keys.shape[1]
    block = math.gcd(stretch_extent, 512)

    def update(index, state):
        top, total, accum = state
        first = index * block
        kk = lax.dynamic_slice_in_dim(keys, first, block, 1).reshape(
            number_entries, block, HEADS, head_dim
        )
        vv = lax.dynamic_slice_in_dim(values, first, block, 1).reshape(
            number_entries, block, HEADS, head_dim
        )
        ok = lax.dynamic_slice_in_dim(okay, first, block, 1)
        bb = lax.dynamic_slice_in_dim(bias_all, first, block, 2)
        score = jnp.einsum("sihd,sjhd->shij", query, kk, preferred_element_type=jnp.float32)
        score = (
            score
            + bb.astype(jnp.float32)[None]
            + ((ok.astype(jnp.float32) - 1.0) * MASK_SCALE)[:, None, None, :]
        )
        newtop = jnp.maximum(top, jnp.max(score, -1))
        probs = jnp.exp(score - newtop[..., None])
        factor = jnp.exp(top - newtop)
        total = total * factor + jnp.sum(probs, -1)
        accum = accum * factor[..., None] + jnp.einsum(
            "shij,sjhd->shid", probs.astype(jnp.bfloat16), vv, preferred_element_type=jnp.float32
        )
        return (newtop, total, accum)

    top, total, accum = lax.fori_loop(0, stretch_extent // block, update, start_state)
    row_mixed = jnp.transpose(accum / total[..., None], (0, 2, 1, 3)).reshape(
        number_entries, homolog_groups, embedding_depth
    )
    lone_head_mixing = (row_mixed * gate).astype(jnp.bfloat16)
    lone_homolog_group = homolog_profile.astype(jnp.float32) + jnp.dot(
        lone_head_mixing, horizontal_final_matrix, preferred_element_type=jnp.float32
    )
    second_activations = standardize_features_fn(lone_homolog_group).astype(jnp.bfloat16)
    column_valid = present_entries.astype(jnp.bfloat16)
    c_query = (
        jnp.dot(second_activations, vertical_asking_matrix, preferred_element_type=jnp.float32)
        * scale
    ).astype(jnp.bfloat16)
    c_query = c_query.reshape(number_entries, homolog_groups, HEADS, head_dim)
    c_keys = jnp.dot(
        second_activations, vertical_lookup_matrix, preferred_element_type=jnp.float32
    ).astype(jnp.bfloat16)
    c_values = jnp.dot(
        second_activations, vertical_content_matrix, preferred_element_type=jnp.float32
    ).astype(jnp.bfloat16)
    c_gate = jax.nn.sigmoid(
        jnp.dot(second_activations, vertical_sigmoid_matrix, preferred_element_type=jnp.float32)
    )
    pieces = (
        lax.all_gather(c_keys, "seq", axis=0, tiled=True),
        lax.all_gather(c_values, "seq", axis=0, tiled=True),
        lax.all_gather(column_valid, "seq", axis=0, tiled=True),
    )
    top_c = jnp.full((homolog_groups, HEADS, number_entries), -1e30, jnp.float32)
    many = pieces[0].shape[0]
    kk = pieces[0].reshape(many, homolog_groups, HEADS, head_dim)
    vv = pieces[1].reshape(many, homolog_groups, HEADS, head_dim)
    masking = ((pieces[2].astype(jnp.float32) - 1.0) * MASK_SCALE).T
    score = (
        jnp.einsum("sihd,tihd->ihst", c_query, kk, preferred_element_type=jnp.float32)
        + masking[:, None, None, :]
    )
    newtop = jnp.maximum(top_c, jnp.max(score, -1))
    probs = jnp.exp(score - newtop[..., None])
    factor = jnp.exp(top_c - newtop)
    total_c = jnp.sum(probs, -1)
    accum_c = jnp.einsum(
        "ihst,tihd->ihsd", probs.astype(jnp.bfloat16), vv, preferred_element_type=jnp.float32
    )
    top_c, total_c, accum_c = (newtop, total_c, accum_c)
    col_mixed = jnp.transpose(accum_c / total_c[..., None], (2, 0, 1, 3)).reshape(
        number_entries, homolog_groups, embedding_depth
    )
    second_mixing = (col_mixed * c_gate).astype(jnp.bfloat16)
    updated_profile = lone_homolog_group + jnp.dot(
        second_mixing, vertical_final_matrix, preferred_element_type=jnp.float32
    )
    x_three = standardize_features_fn(updated_profile).astype(jnp.bfloat16)
    hidden = jax.nn.relu(
        jnp.dot(x_three, widening_matrix, preferred_element_type=jnp.float32)
    ).astype(jnp.bfloat16)
    return (
        updated_profile + jnp.dot(hidden, narrowing_matrix, preferred_element_type=jnp.float32)
    ).astype(jnp.bfloat16)


def solution(mesh):
    placed = (
        P("seq", "res", None),
        P("res", "seq", None),
        P("seq", "res"),
        P("res"),
        P(),
        P(),
        P(),
        P(),
        P(),
        P(),
        P(),
        P(),
        P(),
        P(),
        P(),
        P(),
        P(),
    )
    return jax.shard_map(
        on_device, mesh=mesh, in_specs=placed, out_specs=P("seq", "res", None), check_vma=False
    )
```

profile of v0, /device:TPU:0, one launch (start us, length us, event | category | flops | bytes accessed | tf_op | source)
XLA Modules:
  0.0 310.7 jit_solution(18095125032639848032)
XLA Ops:
  6.6 2.9 convert_reduce_fusion
  9.5 4.1 %fusion.7 = f32[128,64]{1,0:T(8,128)S(1)} fusion(bf16[128,64,128]{2,1,0:T(8,128)(2,1)} %param.18, f32[128,64]{1,0:T(8,128)S(1)} %broadcast_multiply_fusion), kind=kLoop, calls=%fused_computation.10 | loop fusion | flops 4186112 | bytes 2162688 | tf_op jit(solution)/shard_map/reduce_sum | solution.py:19
  13.6 6.2 %fusion.46 = bf16[8,128,64]{2,0,1:T(8,128)(2,1)S(1)} fusion(bf16[128,64,128]{2,1,0:T(8,128)(2,1)S(1)} %copy-done.3, f32[128,64]{1,0:T(8,128)S(1)} %add_rsqrt_fusion, f32[128,64]{1,0:T(8,128)S(1)} %broadcast_multiply_fusion, bf16[128,8]{0,1:T(8,128)(2,1)S(1)} %copy-done.17), kind=kOutput, calls=%fused_computation.55 | convolution fusion | flops 103874560 | bytes 2295808 | tf_op jit(solution)/shard_map/ijc,ch->hij/dot_general | solution.py:45
  22.8 2.2 convolution_convert_fusion.2
  25.8 6.3 %all_gather.23 = bf16[8,512]{1,0:T(8,128)(2,1)S(1)} all-gather(bf16[8,128]{1,0:T(8,128)(2,1)S(1)} %get-tuple-element.26), channel_id=1, replica_groups=mesh['seq'=8,'res'=4] {'res'}, dimensions={1}, use_global_device_ids=true | all-gather | bytes 10240 | tf_op jit(solution)/shard_map/all_gather | solution.py:76
  32.1 31.7 %all-gather.8.cloned.1.call-done = bf16[8,128,512]{1,0,2:T(8,128)(2,1)} async-done(((bf16[8,128,64]{1,0,2:T(8,128)(2,1)}), bf16[8,128,512]{1,0,2:T(8,128)(2,1)}) %all-gather.8.cloned.1.call-update) | async-done | bytes 1048592 | tf_op jit(solution)/shard_map/all_gather | solution.py:51
  65.6 21.1 %all-gather.6.cloned.1.call-done = bf16[8,512,256]{2,1,0:T(8,128)(2,1)} async-done(((bf16[8,128,256]{2,1,0:T(8,128)(2,1)}), bf16[8,512,256]{2,1,0:T(8,128)(2,1)}) %all-gather.6.cloned.1.call-update) | async-done | bytes 2097168 | tf_op jit(solution)/shard_map/all_gather | solution.py:74
  86.7 3.9 %copy.44 = bf16[8,512,256]{1,2,0:T(8,128)(2,1)} copy(bf16[8,512,256]{2,1,0:T(8,128)(2,1)} %all-gather.6.cloned.1.call-done) | data formatting | bytes 4194304 | tf_op jit(solution)/shard_map/all_gather | solution.py:74
  90.6 4.3 %fusion = (f32[8,8,128]{2,1,0:T(8,128)S(1)}, f32[8,8,128,512]{3,2,1,0:T(8,128)S(1)}) fusion(f32[8,512]{1,0:T(8,128)S(1)} %add_multiply_fusion, f32[8,128,512]{2,1,0:T(8,128)S(1)} %copy.46, bf16[8,128,8,32]{1,3,2,0:T(8,128)(2,1)S(1)} %bitcast.89, bf16[8,512,8,32]{1,3,2,0:T(8,128)(2,1)} %bitcast.86), kind=kOutput, calls=%fused_computation.2 | convolution fusion | flops 281010176 | bytes 21544960 | tf_op jit(solution)/shard_map/while/body/eval_jaxpr/sihd,sjhd->shij/dot_general | solution.py:95
  95.0 4.3 %fusion.1 = f32[8,8,128]{2,1,0:T(8,128)S(1)} fusion(f32[8,8,128,512]{3,2,1,0:T(8,128)S(1)} %get-tuple-element.28, f32[8,8,128]{2,1,0:T(8,128)S(1)} %get-tuple-element.24, f32[8,512]{1,0:T(8,128)S(1)} %add_multiply_fusion, f32[8,128,512]{2,1,0:T(8,128)S(1)} %copy.46), kind=kLoop, calls=%fused_computation.3 | loop fusion | flops 16769024 | bytes 18956288 | tf_op jit(solution)/shard_map/while/body/eval_jaxpr/reduce_sum | solution.py:104
  100.9 10.0 %all-gather.10.cloned.1.call-done = bf16[8,512,256]{2,1,0:T(8,128)(2,1)} async-done(((bf16[8,128,256]{2,1,0:T(8,128)(2,1)}), bf16[8,512,256]{2,1,0:T(8,128)(2,1)}) %all-gather.10.cloned.1.call-update) | async-done | bytes 2097168 | tf_op jit(solution)/shard_map/all_gather | solution.py:75
  110.9 3.9 %copy.47 = bf16[8,512,256]{1,2,0:T(8,128)(2,1)} copy(bf16[8,512,256]{2,1,0:T(8,128)(2,1)} %all-gather.10.cloned.1.call-done) | data formatting | bytes 4194304 | tf_op jit(solution)/shard_map/all_gather | solution.py:75
  114.8 9.2 %fusion.40 = f32[8,128,8,32]{1,3,2,0:T(8,128)} fusion(bf16[8,512,8,32]{1,3,2,0:T(8,128)(2,1)} %bitcast.91, f32[8,8,128,512]{3,2,1,0:T(8,128)} %copy-done.1, f32[8,8,128]{2,1,0:T(8,128)S(1)} %get-tuple-element.24, f32[8,512]{1,0:T(8,128)S(1)} %add_multiply_fusion, f32[8,128,512]{2,1,0:T(8,128)S(1)} %copy.46, f32[8,128,8]{1,2,0:T(8,128)S(1)} %bitcast_add_fusion, ...), kind=kOutput, calls=%fused_computation.53 | convolution fusion | flops 285736960 | bytes 22134784 | tf_op jit(solution)/shard_map/while/body/eval_jaxpr/shij,sjhd->shid/dot_general | solution.py:105
  130.3 26.4 %all_gather.26 = bf16[64,128]{1,0:T(8,128)(2,1)S(1)} all-gather(bf16[8,128]{1,0:T(8,128)(2,1)S(1)} %get-tuple-element.25), channel_id=1, replica_groups=mesh['seq'=8,'res'=4] {'seq'}, dimensions={0}, use_global_device_ids=true | all-gather | bytes 18432 | tf_op jit(solution)/shard_map/all_gather | solution.py:137
  157.6 4.0 %copy.51 = bf16[8,128,8,32]{3,0,2,1:T(8,128)(2,1)} copy(bf16[8,128,8,32]{1,3,2,0:T(8,128)(2,1)S(1)} %bitcast.90) | data formatting | bytes 1048576 | tf_op jit(solution)/shard_map/reshape | solution.py:124
  161.6 41.1 %all-gather.12.cloned.1.call-done = bf16[64,128,256]{2,1,0:T(8,128)(2,1)} async-done(((bf16[8,128,256]{2,1,0:T(8,128)(2,1)}), bf16[64,128,256]{2,1,0:T(8,128)(2,1)}) %all-gather.12.cloned.1.call-update) | async-done | bytes 4194320 | tf_op jit(solution)/shard_map/all_gather | solution.py:135
  202.7 9.4 %copy.58 = bf16[64,128,256]{0,2,1:T(8,128)(2,1)} copy(bf16[64,128,256]{2,1,0:T(8,128)(2,1)} %all-gather.12.cloned.1.call-done) | data formatting | bytes 8388608 | tf_op jit(solution)/shard_map/reshape | solution.py:141
  212.1 6.4 %add_reduce_fusion = (f32[128,8,8]{2,1,0:T(8,128)S(1)}, f32[128,8,8,64]{3,2,1,0:T(8,128)S(1)}) fusion(f32[128,64]{1,0:T(8,128)S(1)} %copy.53, bf16[8,128,8,32]{3,0,2,1:T(8,128)(2,1)} %copy.51, bf16[64,128,8,32]{0,3,2,1:T(8,128)(2,1)} %bitcast.85), kind=kOutput, calls=%fused_computation.15 | convolution fusion | flops 34594816 | bytes 6881280 | tf_op jit(solution)/shard_map/sihd,tihd->ihst/dot_general | solution.py:145
  220.4 2.8 fusion.10
  223.2 53.2 %all-gather.14.cloned.1.call-done = bf16[64,128,256]{2,1,0:T(8,128)(2,1)} async-done(((bf16[8,128,256]{2,1,0:T(8,128)(2,1)}), bf16[64,128,256]{2,1,0:T(8,128)(2,1)}) %all-gather.14.cloned.1.call-update) | async-done | bytes 4194320 | tf_op jit(solution)/shard_map/all_gather | solution.py:136
  276.4 9.3 %copy.59 = bf16[64,128,256]{0,2,1:T(8,128)(2,1)} copy(bf16[64,128,256]{2,1,0:T(8,128)(2,1)} %all-gather.14.cloned.1.call-done) | data formatting | bytes 8388608 | tf_op jit(solution)/shard_map/reshape | solution.py:142
  285.6 8.8 %bitcast_divide_fusion = f32[8,128,8,32]{3,0,2,1:T(8,128)} fusion(bf16[64,128,8,32]{0,3,2,1:T(8,128)(2,1)} %bitcast.87, f32[128,8,8,64]{3,2,1,0:T(8,128)} %copy-done.2, f32[8,128,8]{0,2,1:T(8,128)S(1)} %bitcast.93, f32[128,8,8]{2,1,0:T(8,128)S(1)} %broadcast_maximum_fusion, f32[128,64]{1,0:T(8,128)S(1)} %copy.53), kind=kOutput, calls=%fused_computation.12 | convolution fusion | flops 35389440 | bytes 7438336 | tf_op jit(solution)/shard_map/ihst,tihd->ihsd/dot_general | solution.py:152
  294.5 3.8 %copy.56 = f32[8,128,8,32]{1,3,2,0:T(8,128)S(1)} copy(f32[8,128,8,32]{3,0,2,1:T(8,128)} %bitcast_divide_fusion) | data formatting | bytes 2097152 | tf_op jit(solution)/shard_map/div | solution.py:156
  302.0 2.2 fusion.35
  (78 shorter events, 19.9 us)
Async XLA Ops:
  6.5 295.4 %copy-start = (bf16[1024,256]{1,0:T(8,128)(2,1)S(1)}, bf16[1024,256]{1,0:T(8,128)(2,1)}, u32[]{:S(2)}) copy-start(bf16[1024,256]{1,0:T(8,128)(2,1)} %param.33) | copy-start | bytes 1572868
  6.5 7.1 %copy-start.3 = (bf16[128,64,128]{2,1,0:T(8,128)(2,1)S(1)}, bf16[128,64,128]{2,1,0:T(8,128)(2,1)}, u32[]{:S(2)}) copy-start(bf16[128,64,128]{2,1,0:T(8,128)(2,1)} %param.18) | copy-start | bytes 6291460
  6.5 7.1 %copy-start.17 = (bf16[128,8]{0,1:T(8,128)(2,1)S(1)}, bf16[128,8]{0,1:T(8,128)(2,1)}, u32[]{:S(2)}) copy-start(bf16[128,8]{0,1:T(8,128)(2,1)} %param.21) | copy-start | bytes 6148
  6.5 14.3 %copy-start.4 = (bf16[8,128,256]{2,1,0:T(8,128)(2,1)S(1)}, bf16[8,128,256]{2,1,0:T(8,128)(2,1)}, u32[]{:S(2)}) copy-start(bf16[8,128,256]{2,1,0:T(8,128)(2,1)} %param.17) | copy-start | bytes 1572868
  6.5 57.2 %all-gather.8.cloned.1.call-start = ((), (), s32[]{:S(2)}) async-start(), calls=%async_computation.1 | async-start | bytes 1179648 | tf_op jit(solution)/shard_map/all_gather | solution.py:51
  9.5 11.9 %copy-start.12 = (bf16[256,256]{1,0:T(8,128)(2,1)S(1)}, bf16[256,256]{1,0:T(8,128)(2,1)}, u32[]{:S(2)}) copy-start(bf16[256,256]{1,0:T(8,128)(2,1)} %param.23) | copy-start | bytes 393220
  19.8 5.2 %copy-start.13 = (bf16[256,256]{1,0:T(8,128)(2,1)S(1)}, bf16[256,256]{1,0:T(8,128)(2,1)}, u32[]{:S(2)}) copy-start(bf16[256,256]{1,0:T(8,128)(2,1)} %param.22) | copy-start | bytes 393220
  19.8 5.9 %copy-start.9 = (s32[8,128]{1,0:T(8,128)S(1)}, s32[8,128]{1,0:T(8,128)}, u32[]{:S(2)}) copy-start(s32[8,128]{1,0:T(8,128)} %param.19) | copy-start | bytes 12292
  19.8 5.9 %copy-start.10 = (s32[128]{0:T(128)S(1)}, s32[128]{0:T(128)}, u32[]{:S(2)}) copy-start(s32[128]{0:T(128)} %param.20) | copy-start | bytes 1540
  20.7 65.9 %all-gather.6.cloned.1.call-start = ((), (), s32[]{:S(2)}) async-start(), calls=%async_computation | async-start | bytes 2621440 | tf_op jit(solution)/shard_map/all_gather | solution.py:74
  22.7 88.2 %all-gather.10.cloned.1.call-start = ((), (), s32[]{:S(2)}) async-start(), calls=%async_computation.2 | async-start | bytes 2621440 | tf_op jit(solution)/shard_map/all_gather | solution.py:75
  24.9 177.7 %all-gather.12.cloned.1.call-start = ((), (), s32[]{:S(2)}) async-start(), calls=%async_computation.3 | async-start | bytes 4718592 | tf_op jit(solution)/shard_map/all_gather | solution.py:135
  94.9 5.9 %copy-start.1 = (f32[8,8,128,512]{3,2,1,0:T(8,128)}, f32[8,8,128,512]{3,2,1,0:T(8,128)S(1)}, u32[]{:S(2)}) copy-start(f32[8,8,128,512]{3,2,1,0:T(8,128)S(1)} %get-tuple-element.28) | copy-start | bytes 50331652
  114.8 10.8 %copy-start.5 = (bf16[8,128,256]{2,1,0:T(8,128)(2,1)S(1)}, bf16[8,128,256]{2,1,0:T(8,128)(2,1)}, u32[]{:S(2)}) copy-start(bf16[8,128,256]{2,1,0:T(8,128)(2,1)} %param.17) | copy-start | bytes 1572868
  114.8 10.8 %copy-start.14 = (bf16[256,256]{1,0:T(8,128)(2,1)S(1)}, bf16[256,256]{1,0:T(8,128)(2,1)}, u32[]{:S(2)}) copy-start(bf16[256,256]{1,0:T(8,128)(2,1)} %param.26) | copy-start | bytes 393220
  125.6 2.1 copy-start.6
  125.6 3.4 %copy-start.7 = (bf16[256,256]{1,0:T(8,128)(2,1)S(1)}, bf16[256,256]{1,0:T(8,128)(2,1)}, u32[]{:S(2)}) copy-start(bf16[256,256]{1,0:T(8,128)(2,1)} %param.29) | copy-start | bytes 393220
  127.2 29.6 %copy-start.8 = (bf16[256,256]{1,0:T(8,128)(2,1)S(1)}, bf16[256,256]{1,0:T(8,128)(2,1)}, u32[]{:S(2)}) copy-start(bf16[256,256]{1,0:T(8,128)(2,1)} %param.27) | copy-start | bytes 393220
  128.9 147.4 %all-gather.14.cloned.1.call-start = ((), (), s32[]{:S(2)}) async-start(), calls=%async_computation.4 | async-start | bytes 4718592 | tf_op jit(solution)/shard_map/all_gather | solution.py:136
  218.5 1.9 copy-start.2
  294.5 5.1 %copy-start.15 = (bf16[256,256]{1,0:T(8,128)(2,1)S(1)}, bf16[256,256]{1,0:T(8,128)(2,1)}, u32[]{:S(2)}) copy-start(bf16[256,256]{1,0:T(8,128)(2,1)} %param.31) | copy-start | bytes 393220
  294.5 5.1 %copy-start.16 = (bf16[256,256]{1,0:T(8,128)(2,1)S(1)}, bf16[256,256]{1,0:T(8,128)(2,1)}, u32[]{:S(2)}) copy-start(bf16[256,256]{1,0:T(8,128)(2,1)} %param.30) | copy-start | bytes 393220
  299.6 2.4 copy-start.11
Sparse Core Ops, SparseCore 0:
  20.9 42.8 all-gather.7
  65.3 21.3 all-gather.5
  88.2 22.5 all-gather.9
  129.1 73.5 all-gather.11
  204.7 71.6 all-gather.13
where the time goes:
time: 312 us; the launch traced here: 311 us
  waiting for transfers between devices  157 us (50%)
  matrix products  47.6 us (15%)
  local copies, waits for them, and re-layouts  44.1 us (14%)
  blocking collectives  32.7 us (10%)
  other arithmetic  15.5 us (5%)
  between operations  13.5 us (4%)
    all_gather x1, waiting for transfers between devices, on_device(): lax.all_gather(c_values, 'seq', axis=0, tiled=True)  53.2 us
    all_gather x1, waiting for transfers between devices, on_device(): lax.all_gather(c_keys, 'seq', axis=0, tiled=True)  41.1 us
    all_gather x1, waiting for transfers between devices, on_device(): bias_all = lax.all_gather(bias, 'seq', axis=2, tiled=True)  31.7 us
    all_gather x1, blocking collectives, on_device(): lax.all_gather(column_valid, 'seq', axis=0, tiled=True)  26.4 us
    all_gather x1, waiting for transfers between devices, on_device(): lax.all_gather(keys, 'res', axis=1, tiled=True)  21.1 us
    all_gather x1, waiting for transfers between devices, on_device(): lax.all_gather(values, 'res', axis=1, tiled=True)  9.98 us
    reshape x1, local copies, waits for them, and re-layouts, on_device(): kk = pieces[0].reshape(many, homolog_groups, HEADS, head_dim)  9.37 us
    reshape x1, local copies, waits for them, and re-layouts, on_device(): vv = pieces[1].reshape(many, homolog_groups, HEADS, head_dim)  9.28 us
  transfers between devices with their start and end apart: 5, of which 5 were waited for; matrix products, arithmetic and copies ran while one was open for 14% of the time, Pallas kernels for 0%

commit v1 on v0

v1 whole, which is shorter than its diff:
```python
import functools

import jax
import jax.numpy as jnp
from jax import lax
from jax.experimental import pallas as pl
from jax.experimental.pallas import tpu as pltpu
from jax.sharding import PartitionSpec as P

HEADS = 8
HEAD_DIM = 32
EPS = 1e-05
MASK_SCALE = 1000000000.0
MESH = pl.DeviceIdType.MESH
BF16 = jnp.bfloat16
F32 = jnp.float32


def norm(v):
    center = v - jnp.mean(v, -1, keepdims=True)
    spread = jnp.mean(center * center, -1, keepdims=True)
    return center * lax.rsqrt(spread + EPS)


def mm(a, b):
    return jnp.dot(a, b, preferred_element_type=F32)


def mm_t(a, b):
    return lax.dot_general(a, b, (((1,), (1,)), ((), ())), preferred_element_type=F32)


def head_mask(rows, channels, h):
    lane = lax.broadcasted_iota(jnp.int32, (rows, channels), 1)
    return (lane >= h * HEAD_DIM) & (lane < (h + 1) * HEAD_DIM)


class Gather:
    def __init__(self, axis, n, buf, send, recv):
        self.axis, self.n, self.buf, self.send, self.recv = axis, n, buf, send, recv
        self.me = lax.axis_index(axis)
        self.sib = self.me + 1 - 2 * lax.rem(self.me, 2)
        self.far = n // 2 - 1

    def copy(self, slot, sem, to):
        return pltpu.make_async_remote_copy(
            src_ref=self.buf.at[slot],
            dst_ref=self.buf.at[slot],
            send_sem=self.send.at[sem],
            recv_sem=self.recv.at[slot],
            device_id={self.axis: to},
            device_id_type=MESH,
        )

    def source(self, t):
        return lax.rem(self.me + self.n - 2 * t, self.n)

    def start(self):
        for t in range(1, self.far + 1):
            self.copy(self.me, t, lax.rem(self.me + 2 * t, self.n)).start()
        self.copy(self.me, 0, self.sib).start()

    def forward(self, t):
        src = self.source(t)
        c = self.copy(src, self.far + t, self.sib)
        c.wait_recv()
        c.start()

    def finish(self, t):
        src = lax.rem(self.sib + self.n - 2 * t, self.n)
        self.copy(src, 0, self.sib).wait_recv()
        return src

    def drain(self):
        for t in range(2 * self.far + 1):
            self.copy(self.me, t, self.sib).wait_send()


def kernel(
    n_seq,
    n_res,
    hp,
    cp,
    present,
    resolved,
    wz,
    wq,
    wk,
    wv,
    wg,
    wo,
    cq,
    ck,
    cv,
    cg,
    co,
    wide,
    narrow,
    out,
    prof,
    rmask,
    cmask,
    cmask_t,
    bstage,
    brecv,
    ball,
    q1,
    g1,
    k1,
    v1,
    m1b,
    x2s,
    x2t,
    xf,
    q2,
    k2,
    v2,
    g2,
    af,
    a2s,
    a2r,
    prof_send,
    prof_recv,
    rm_send,
    rm_recv,
    cm_send,
    cm_recv,
    b_send,
    b_recv,
    f_send,
    f_recv,
    r_send,
    r_recv,
):
    entries, groups, depth = hp.shape
    parts, rows, jb, _ = cp.shape
    ni = groups // n_seq
    many = n_seq * entries
    scale = HEAD_DIM ** (-0.5)
    me = lax.axis_index("seq")
    mine = lax.axis_index("res")

    barrier = pltpu.get_barrier_semaphore()
    for t in range(1, n_seq):
        pl.semaphore_signal(
            barrier, inc=1, device_id={"seq": lax.rem(me + t, n_seq)}, device_id_type=MESH
        )
    for t in range(1, n_res):
        pl.semaphore_signal(
            barrier, inc=1, device_id={"res": lax.rem(mine + t, n_res)}, device_id_type=MESH
        )

    prof[mine] = hp[...]
    here = present[...]
    rmask[mine] = ((here * resolved[...]).astype(F32) - 1.0) * MASK_SCALE
    cmask[me] = (here.astype(F32) - 1.0) * MASK_SCALE
    pl.semaphore_wait(barrier, n_seq - 1 + n_res - 1)

    gp = Gather("res", n_res, prof, prof_send, prof_recv)
    gr = Gather("res", n_res, rmask, rm_send, rm_recv)
    gc = Gather("seq", n_seq, cmask, cm_send, cm_recv)
    gb = Gather("seq", n_seq, brecv, b_send, b_recv)
    gr.start()
    gc.start()
    gp.start()

    step = 8

    def bias_block(b, carry):
        wide_rows = cp[:, pl.ds(b * step, step)].astype(F32)
        x = norm(wide_rows.reshape(parts * step * jb, wide_rows.shape[-1]))
        x = x.reshape(parts, step, jb, x.shape[-1])
        high = x.astype(BF16)
        low = (x - high.astype(F32)).astype(BF16)
        for k in range(step):
            hi = jnp.concatenate([high[a, k] for a in range(parts)], 0)
            lo = jnp.concatenate([low[a, k] for a in range(parts)], 0)
            piece = mm_t(wz[...], hi) + mm_t(wz[...], lo)
            bstage[pl.ds(b * step + k, HEADS, stride=rows), :] = piece[:HEADS]
        return carry

    lax.fori_loop(0, rows // step, bias_block, 0)
    brecv[me] = bstage[...].astype(BF16)
    gb.start()

    def own_side(s, carry):
        x = norm(hp[s].astype(F32)).astype(BF16)
        q1[s] = (mm(x, wq[...]) * scale).astype(BF16)
        g1[s] = jax.nn.sigmoid(mm(x, wg[...]))
        return carry

    lax.fori_loop(0, entries, own_side, 0)

    def key_side(r):
        start = pl.multiple_of(r * groups, groups)

        def one(s, carry):
            x = norm(prof[r, s].astype(F32)).astype(BF16)
            k1[s, pl.ds(start, groups), :] = mm(x, wk[...]).astype(BF16)
            v1[s, pl.ds(start, groups), :] = mm(x, wv[...]).astype(BF16)
            return carry

        lax.fori_loop(0, entries, one, 0)

    key_side(mine)
    if gb.far >= 1:
        gb.forward(1)
    for t in range(1, gp.far + 1):
        gr.forward(t)
        gp.forward(t)
    for t in range(2, gb.far + 1):
        gb.forward(t)
    for t in range(1, gc.far + 1):
        gc.forward(t)
    for t in range(1, gp.far + 1):
        key_side(gp.source(t))
    for t in range(0, gp.far + 1):
        key_side(gp.finish(t))
        gr.finish(t)
    for t in range(0, gc.far + 1):
        gc.finish(t)
    for t in range(0, gb.far + 1):
        gb.finish(t)

    cmask_t[...] = jnp.transpose(cmask[...].reshape(many, groups))

    if parts == 2:
        first = lax.broadcasted_iota(jnp.int32, (rows, 2 * jb), 1) < jb
        for h in range(HEADS):
            for c in range(n_seq // 2):
                left = brecv[2 * c, h * rows : (h + 1) * rows, :].astype(F32)
                right = brecv[2 * c + 1, h * rows : (h + 1) * rows, :].astype(F32)
                top = jnp.where(first, left, pltpu.roll(right, jb, 1))
                low = jnp.where(first, pltpu.roll(left, jb, 1), right)
                cols = slice(c * 2 * jb, (c + 1) * 2 * jb)
                ball[h, :rows, cols] = top.astype(BF16)
                ball[h, rows:, cols] = low.astype(BF16)

    def bias_of(h):
        if parts == 2:
            return ball[h].astype(F32)
        return jnp.concatenate(
            [brecv[c, h * rows : (h + 1) * rows, :] for c in range(n_seq)], 1
        ).astype(F32)

    hmask = [head_mask(groups, depth, h) for h in range(HEADS)]

    def row(s, carry):
        q = q1[s]
        kk = k1[s]
        vv = v1[s]
        masking = jnp.concatenate([rmask[r, pl.ds(s, 1), :] for r in range(n_res)], 1)
        acc = jnp.zeros((groups, depth), F32)
        for h in range(HEADS):
            qh = jnp.where(hmask[h], q, jnp.zeros_like(q))
            score = mm_t(qh, kk) + bias_of(h) + masking
            probs = jnp.exp(score - jnp.max(score, -1, keepdims=True))
            total = jnp.sum(probs, -1, keepdims=True)
            mixed = mm(probs.astype(BF16), vv)
            acc = jnp.where(hmask[h], mixed / total, acc)
        a1 = (acc * g1[s]).astype(BF16)
        m1 = hp[s].astype(F32) + mm(a1, wo[...])
        x2 = norm(m1)
        for p in range(n_seq):
            m1b[p, s] = m1[p * ni : (p + 1) * ni]
            x2s[p, s] = x2[p * ni : (p + 1) * ni].astype(BF16)
        for t in range(1, n_seq):
            to = lax.rem(me + t, n_seq)
            pltpu.make_async_remote_copy(
                src_ref=x2s.at[to, s],
                dst_ref=x2t.at[me, s],
                send_sem=f_send.at[t],
                recv_sem=f_recv.at[me],
                device_id={"seq": to},
                device_id_type=MESH,
            ).start()
        return carry

    lax.fori_loop(0, entries, row, 0)

    def whole_copy(t, src, dst, send, recv):
        origin = lax.rem(me + n_seq - t, n_seq)
        to = lax.rem(me + t, n_seq)
        return pltpu.make_async_remote_copy(
            src_ref=src.at[to],
            dst_ref=dst.at[origin],
            send_sem=send.at[t],
            recv_sem=recv.at[origin],
            device_id={"seq": to},
            device_id_type=MESH,
        )

    x2t[me] = x2s[me]
    for t in range(1, n_seq):
        whole_copy(t, x2s, x2t, f_send, f_recv).wait_recv()

    half = 128
    halves = depth // half
    for c in range(n_seq):
        x = x2t[c].astype(F32).reshape(entries * ni, depth)
        for e in range(halves):
            xf[e, c * entries * ni : (c + 1) * entries * ni, :] = x[:, e * half : (e + 1) * half]

    for i in range(ni):
        x = jnp.concatenate(
            [xf[e, pl.ds(i, many, stride=ni), :] for e in range(halves)], 1
        ).astype(BF16)
        q2[i] = (mm(x, cq[...]) * scale).astype(BF16)
        k2[i] = mm(x, ck[...]).astype(BF16)
        v2[i] = mm(x, cv[...]).astype(BF16)
        g2[i] = jax.nn.sigmoid(mm(x, cg[...]))

    cm = [head_mask(many, depth, h) for h in range(HEADS)]

    def column(i, carry):
        q = q2[i]
        masking = cmask_t[pl.ds(me * ni + i, 1), :]
        stacked = jnp.concatenate([jnp.where(m, q, jnp.zeros_like(q)) for m in cm], 0)
        score = mm_t(stacked, k2[i]) + masking
        probs = jnp.exp(score - jnp.max(score, -1, keepdims=True))
        total = jnp.sum(probs, -1, keepdims=True)
        mixed = mm(probs.astype(BF16), v2[i]) / total
        acc = mixed[:many]
        for h in range(1, HEADS):
            acc = jnp.where(cm[h], mixed[h * many : (h + 1) * many], acc)
        acc = acc * g2[i]
        for e in range(halves):
            af[e, pl.ds(pl.multiple_of(i * many, many), many), :] = acc[:, e * half : (e + 1) * half]
        return carry

    lax.fori_loop(0, ni, column, 0)

    for s in range(many):
        x = jnp.concatenate(
            [af[e, pl.ds(s, ni, stride=many), :] for e in range(halves)], 1
        )
        a2s[s // entries, s % entries] = x.astype(BF16)

    for t in range(1, n_seq):
        to = lax.rem(me + t, n_seq)
        pltpu.make_async_remote_copy(
            src_ref=a2s.at[to],
            dst_ref=a2r.at[me],
            send_sem=r_send.at[t],
            recv_sem=r_recv.at[me],
            device_id={"seq": to},
            device_id_type=MESH,
        ).start()
    a2r[me] = a2s[me]
    for t in range(1, n_seq):
        whole_copy(t, a2s, a2r, r_send, r_recv).wait_recv()

    pair = 2
    for c in range(0, n_seq, pair):
        a2 = a2r[c : c + pair].astype(F32).reshape(pair * entries * ni, depth).astype(BF16)
        m2 = m1b[c : c + pair].reshape(pair * entries * ni, depth) + mm(a2, co[...])
        x3 = norm(m2).astype(BF16)
        hid = jnp.maximum(mm(x3, wide[...]), 0.0).astype(BF16)
        res = (m2 + mm(hid, narrow[...])).reshape(pair, entries, ni, depth)
        for e in range(pair):
            out[:, (c + e) * ni : (c + e + 1) * ni, :] = res[e].astype(BF16)

    for g in (gp, gr, gc, gb):
        g.drain()
    for t in range(1, n_seq):
        whole_copy(t, x2s, x2t, f_send, f_recv).wait_send()
        whole_copy(t, a2s, a2r, r_send, r_recv).wait_send()


def on_device(n_seq, n_res, hp, cp, present, resolved, wz, *weights):
    entries, groups, depth = hp.shape
    jb = cp.shape[1]
    parts = 128 // jb
    rows = groups // parts
    total = n_res * groups
    ni = groups // n_seq
    many = n_seq * entries
    vm = pltpu.VMEM
    dma = pltpu.SemaphoreType.DMA
    scratch = [
        vm((n_res, entries, groups, depth), BF16),
        vm((n_res, entries, groups), F32),
        vm((n_seq, entries, groups), F32),
        vm((groups, many), F32),
        vm((HEADS * rows, 128), F32),
        vm((n_seq, HEADS * rows, 128), BF16),
        vm((HEADS, groups, total) if parts == 2 else (1, 16, 128), BF16),
        vm((entries, groups, depth), BF16),
        vm((entries, groups, depth), F32),
        vm((entries, total, depth), BF16),
        vm((entries, total, depth), BF16),
        vm((n_seq, entries, ni, depth), F32),
        vm((n_seq, entries, ni, depth), BF16),
        vm((n_seq, entries, ni, depth), BF16),
        vm((depth // 128, many * ni, 128), F32),
        vm((ni, many, depth), BF16),
        vm((ni, many, depth), BF16),
        vm((ni, many, depth), BF16),
        vm((ni, many, depth), F32),
        vm((depth // 128, many * ni, 128), F32),
        vm((n_seq, entries, ni, depth), BF16),
        vm((n_seq, entries, ni, depth), BF16),
    ]
    for n in (n_res, n_res, n_seq, n_seq, n_seq, n_seq):
        scratch += [dma((n,)), dma((n,))]
    operands = (
        hp,
        cp.reshape(parts, rows, jb, cp.shape[-1]),
        present,
        resolved.reshape(1, groups),
        jnp.pad(wz.T, ((0, 8), (0, 0))),
        *weights,
    )
    spec = pl.BlockSpec(memory_space=pltpu.VMEM)
    return pl.pallas_call(
        functools.partial(kernel, n_seq, n_res),
        out_shape=jax.ShapeDtypeStruct(hp.shape, BF16),
        in_specs=[spec] * len(operands),
        out_specs=spec,
        scratch_shapes=scratch,
        compiler_params=pltpu.CompilerParams(
            collective_id=0, has_side_effects=True, vmem_limit_bytes=60 * 1024 * 1024
        ),
    )(*operands)


def solution(mesh):
    placed = (P("seq", "res", None), P("res", "seq", None), P("seq", "res"), P("res"))
    return jax.shard_map(
        functools.partial(on_device, mesh.shape["seq"], mesh.shape["res"]),
        mesh=mesh,
        in_specs=placed + (P(),) * 13,
        out_specs=P("seq", "res", None),
        check_vma=False,
    )
```

time: 312 us -> 88.3 us (0.28)
  waiting for transfers between devices: 157 us -> 0 us
  Pallas kernels: 0 us -> 84.9 us
  matrix products: 47.6 us -> 0 us
  local copies, waits for them, and re-layouts: 44.1 us -> 3.14 us
  blocking collectives: 32.7 us -> 0 us
  other arithmetic: 15.5 us -> 0 us
  between operations: 13.5 us -> 0.01 us
    all_gather x5 -> x0, waiting for transfers between devices: 157 us -> none  [the longest x1 53.2 us: on_device(): lax.all_gather(c_values, 'seq', axis=0, tiled=True)]
    pallas_call x0 -> x1, Pallas kernels: none -> 84.9 us  [on_device(): pl.pallas_call(functools.partial(kernel, n_seq, n_res), out_shape=jax.Sha...]
    dot_general x14 -> x0, matrix products: 47.6 us -> none  [the longest x1 9.21 us: update(): jnp.einsum('shij,sjhd->shid', probs.astype(jnp.bfloat16), vv, preferred_e...]
    all_gather x2 -> x0, blocking collectives: 32.7 us -> none  [the longest x1 26.4 us: on_device(): lax.all_gather(column_valid, 'seq', axis=0, tiled=True)]
    reshape x5 -> x0, local copies, waits for them, and re-layouts: 25.5 us -> none  [the longest x1 9.37 us: on_device(): kk = pieces[0].reshape(many, homolog_groups, HEADS, head_dim)]
    reduce_sum x8 -> x0, other arithmetic: 15.3 us -> none  [the longest x4 5.19 us: standardize_features_fn(): spread = jnp.mean(center * center, -1, keepdims=True)]
    all_gather x2 -> x0, local copies, waits for them, and re-layouts: 7.82 us -> none  [the longest x1 3.91 us: on_device(): lax.all_gather(values, 'res', axis=1, tiled=True)]
    div x1 -> x0, local copies, waits for them, and re-layouts: 3.79 us -> none  [on_device(): accum_c / total_c[..., None]]
  transfers between devices with their start and end apart: 5 -> 0, of which waited for: 5 -> 0; matrix products, arithmetic and copies ran while one was open for 14% -> 0% of each run, Pallas kernels for 0% -> 0%
where the time goes in v1:
time: 88.3 us; the launch traced here: 88 us
  Pallas kernels  84.9 us (96%)
  local copies, waits for them, and re-layouts  3.14 us (4%)
    pallas_call x1, Pallas kernels, on_device(): pl.pallas_call(functools.partial(kernel, n_seq, n_res), out_shape=jax.Sha...  84.9 us
    unnamed x1, local copies, waits for them, and re-layouts  1.87 us

profile of v1, /device:TPU:0, one launch (start us, length us, event | category | flops | bytes accessed | tf_op | source)
XLA Modules:
  0.0 88.0 jit_solution(4817652907206358361)
XLA Ops:
  0.0 1.3 %pad.4.wz = bf16[16,128]{1,0:T(8,128)(2,1)} pad(bf16[8,128]{1,0:T(8,128)(2,1)} %bitcast.4, bf16[]{:T(256)} %constant.2.clone.1), padding=0_8x0_0 | pad | bytes 6146 | tf_op jit(solution)/shard_map/jit(_pad)/pad | solution.py:411
  1.3 84.9 %shard_map.163 = bf16[8,128,256]{2,1,0:T(8,128)(2,1)} custom-call(bf16[8,128,256]{2,1,0:T(8,128)(2,1)} %hp.1, bf16[2,64,64,128]{3,2,1,0:T(8,128)(2,1)} %bitcast.3, s32[8,128]{1,0:T(8,128)} %present.1, s32[1,128]{1,0:T(1,128)} %bitcast.5, bf16[16,128]{1,0:T(8,128)(2,1)} %pad.4.wz, bf16[256,256]{1,0:T(8,128)(2,1)} %wq.1, bf16[256,256]{1,0:T(8,128)(2,1)} %wk.1, ...), custom_call_target="tpu_custom_call" | custom-call | tf_op jit(solution)/shard_map/pallas_call | solution.py:415
  86.2 1.9 %copy.19 = bf16[8,128,256]{2,1,0:T(8,128)(2,1)} copy(bf16[8,128,256]{2,1,0:T(8,128)(2,1)} %shard_map.163) | data formatting | bytes 1048576

commit v2 on v1

--- a/solution.py
+++ b/solution.py
@@ -11,6 +11,8 @@
 HEAD_DIM = 32
 EPS = 1e-05
 MASK_SCALE = 1000000000.0
+CHUNKS = 2
+TOGETHER = 4
 MESH = pl.DeviceIdType.MESH
 BF16 = jnp.bfloat16
 F32 = jnp.float32
@@ -116,7 +118,6 @@
     k2,
     v2,
     g2,
-    af,
     a2s,
     a2r,
     prof_send,
@@ -137,6 +138,8 @@
     ni = groups // n_seq
     many = n_seq * entries
     scale = HEAD_DIM ** (-0.5)
+    half = 128
+    halves = depth // half
     me = lax.axis_index("seq")
     mine = lax.axis_index("res")
 
@@ -159,29 +162,34 @@
     gp = Gather("res", n_res, prof, prof_send, prof_recv)
     gr = Gather("res", n_res, rmask, rm_send, rm_recv)
     gc = Gather("seq", n_seq, cmask, cm_send, cm_recv)
-    gb = Gather("seq", n_seq, brecv, b_send, b_recv)
+    gbs = [
+        Gather("seq", n_seq, brecv.at[a], b_send.at[a], b_recv.at[a]) for a in range(CHUNKS)
+    ]
     gr.start()
     gc.start()
     gp.start()
 
     step = 8
-
-    def bias_block(b, carry):
-        wide_rows = cp[:, pl.ds(b * step, step)].astype(F32)
+    some = rows // CHUNKS
+    wzt = jnp.transpose(wz[...].astype(F32)).astype(BF16)
+
+    def bias_block(a, b, carry):
+        wide_rows = cp[:, pl.ds(a * some + b * step, step)].astype(F32)
         x = norm(wide_rows.reshape(parts * step * jb, wide_rows.shape[-1]))
         x = x.reshape(parts, step, jb, x.shape[-1])
         high = x.astype(BF16)
         low = (x - high.astype(F32)).astype(BF16)
         for k in range(step):
-            hi = jnp.concatenate([high[a, k] for a in range(parts)], 0)
-            lo = jnp.concatenate([low[a, k] for a in range(parts)], 0)
-            piece = mm_t(wz[...], hi) + mm_t(wz[...], lo)
-            bstage[pl.ds(b * step + k, HEADS, stride=rows), :] = piece[:HEADS]
+            hi = jnp.concatenate([high[e, k] for e in range(parts)], 0)
+            lo = jnp.concatenate([low[e, k] for e in range(parts)], 0)
+            piece = mm_t(wzt, hi) + mm_t(wzt, lo)
+            bstage[pl.ds(b * step + k, HEADS, stride=some), :] = piece
         return carry
 
-    lax.fori_loop(0, rows // step, bias_block, 0)
-    brecv[me] = bstage[...].astype(BF16)
-    gb.start()
+    for a in range(CHUNKS):
+        lax.fori_loop(0, some // step, functools.partial(bias_block, a), 0)
+        brecv[a, me] = bstage[...].astype(BF16)
+        gbs[a].start()
 
     def own_side(s, carry):
         x = norm(hp[s].astype(F32)).astype(BF16)
@@ -203,13 +211,13 @@
         lax.fori_loop(0, entries, one, 0)
 
     key_side(mine)
-    if gb.far >= 1:
-        gb.forward(1)
+    for t in range(1, gbs[0].far + 1):
+        gbs[0].forward(t)
     for t in range(1, gp.far + 1):
         gr.forward(t)
         gp.forward(t)
-    for t in range(2, gb.far + 1):
-        gb.forward(t)
+    for t in range(1, gbs[1].far + 1):
+        gbs[1].forward(t)
     for t in range(1, gc.far + 1):
         gc.forward(t)
     for t in range(1, gp.far + 1):
@@ -219,28 +227,36 @@
         gr.finish(t)
     for t in range(0, gc.far + 1):
         gc.finish(t)
-    for t in range(0, gb.far + 1):
-        gb.finish(t)
+    for gb in gbs:
+        for t in range(0, gb.far + 1):
+            gb.finish(t)
 
     cmask_t[...] = jnp.transpose(cmask[...].reshape(many, groups))
 
     if parts == 2:
-        first = lax.broadcasted_iota(jnp.int32, (rows, 2 * jb), 1) < jb
+        first = lax.broadcasted_iota(jnp.int32, (some, 2 * jb), 1) < jb
         for h in range(HEADS):
             for c in range(n_seq // 2):
-                left = brecv[2 * c, h * rows : (h + 1) * rows, :].astype(F32)
-                right = brecv[2 * c + 1, h * rows : (h + 1) * rows, :].astype(F32)
-                top = jnp.where(first, left, pltpu.roll(right, jb, 1))
-                low = jnp.where(first, pltpu.roll(left, jb, 1), right)
                 cols = slice(c * 2 * jb, (c + 1) * 2 * jb)
-                ball[h, :rows, cols] = top.astype(BF16)
-                ball[h, rows:, cols] = low.astype(BF16)
+                for a in range(CHUNKS):
+                    left = brecv[a, 2 * c, h * some : (h + 1) * some, :].astype(F32)
+                    right = brecv[a, 2 * c + 1, h * some : (h + 1) * some, :].astype(F32)
+                    top = jnp.where(first, left, pltpu.roll(right, jb, 1))
+                    low = jnp.where(first, pltpu.roll(left, jb, 1), right)
+                    ball[h, a * some : (a + 1) * some, cols] = top.astype(BF16)
+                    ball[h, rows + a * some : rows + (a + 1) * some, cols] = low.astype(BF16)
 
     def bias_of(h):
         if parts == 2:
             return ball[h].astype(F32)
         return jnp.concatenate(
-            [brecv[c, h * rows : (h + 1) * rows, :] for c in range(n_seq)], 1
+            [
+                jnp.concatenate(
+                    [brecv[a, c, h * some : (h + 1) * some, :] for c in range(n_seq)], 1
+                )
+                for a in range(CHUNKS)
+            ],
+            0,
         ).astype(F32)
 
     hmask = [head_mask(groups, depth, h) for h in range(HEADS)]
@@ -251,18 +267,29 @@
         vv = v1[s]
         masking = jnp.concatenate([rmask[r, pl.ds(s, 1), :] for r in range(n_res)], 1)
         acc = jnp.zeros((groups, depth), F32)
-        for h in range(HEADS):
-            qh = jnp.where(hmask[h], q, jnp.zeros_like(q))
-            score = mm_t(qh, kk) + bias_of(h) + masking
-            probs = jnp.exp(score - jnp.max(score, -1, keepdims=True))
-            total = jnp.sum(probs, -1, keepdims=True)
-            mixed = mm(probs.astype(BF16), vv)
-            acc = jnp.where(hmask[h], mixed / total, acc)
+        for first_head in range(0, HEADS, TOGETHER):
+            heads = range(first_head, first_head + TOGETHER)
+            stacked = jnp.concatenate(
+                [jnp.where(hmask[h], q, jnp.zeros_like(q)) for h in heads], 0
+            )
+            scores = mm_t(stacked, kk)
+            weights, inverses = [], []
+            for e, h in enumerate(heads):
+                score = scores[e * groups : (e + 1) * groups] + bias_of(h) + masking
+                probs = jnp.exp(score - jnp.max(score, -1, keepdims=True))
+                inverses.append(1.0 / jnp.sum(probs, -1, keepdims=True))
+                weights.append(probs.astype(BF16))
+            mixed = mm(jnp.concatenate(weights, 0), vv)
+            for e, h in enumerate(heads):
+                acc = jnp.where(
+                    hmask[h], mixed[e * groups : (e + 1) * groups] * inverses[e], acc
+                )
         a1 = (acc * g1[s]).astype(BF16)
         m1 = hp[s].astype(F32) + mm(a1, wo[...])
         x2 = norm(m1)
+        for e in range(halves):
+            m1b[e, pl.ds(s, groups, stride=entries), :] = m1[:, e * half : (e + 1) * half]
         for p in range(n_seq):
-            m1b[p, s] = m1[p * ni : (p + 1) * ni]
             x2s[p, s] = x2[p * ni : (p + 1) * ni].astype(BF16)
         for t in range(1, n_seq):
             to = lax.rem(me + t, n_seq)
@@ -294,73 +321,80 @@
     for t in range(1, n_seq):
         whole_copy(t, x2s, x2t, f_send, f_recv).wait_recv()
 
-    half = 128
-    halves = depth // half
     for c in range(n_seq):
         x = x2t[c].astype(F32).reshape(entries * ni, depth)
         for e in range(halves):
             xf[e, c * entries * ni : (c + 1) * entries * ni, :] = x[:, e * half : (e + 1) * half]
 
-    for i in range(ni):
-        x = jnp.concatenate(
-            [xf[e, pl.ds(i, many, stride=ni), :] for e in range(halves)], 1
-        ).astype(BF16)
-        q2[i] = (mm(x, cq[...]) * scale).astype(BF16)
-        k2[i] = mm(x, ck[...]).astype(BF16)
-        v2[i] = mm(x, cv[...]).astype(BF16)
-        g2[i] = jax.nn.sigmoid(mm(x, cg[...]))
+    x = jnp.concatenate(
+        [
+            jnp.concatenate([xf[e, pl.ds(i, many, stride=ni), :] for e in range(halves)], 1)
+            for i in range(ni)
+        ],
+        0,
+    ).astype(BF16)
+    q2[...] = (mm(x, cq[...]) * scale).astype(BF16).reshape(q2.shape)
+    k2[...] = mm(x, ck[...]).astype(BF16).reshape(k2.shape)
+    v2[...] = mm(x, cv[...]).astype(BF16).reshape(v2.shape)
+    g2[...] = jax.nn.sigmoid(mm(x, cg[...])).reshape(g2.shape)
 
     cm = [head_mask(many, depth, h) for h in range(HEADS)]
 
-    def column(i, carry):
+    def column(i):
         q = q2[i]
         masking = cmask_t[pl.ds(me * ni + i, 1), :]
         stacked = jnp.concatenate([jnp.where(m, q, jnp.zeros_like(q)) for m in cm], 0)
         score = mm_t(stacked, k2[i]) + masking
         probs = jnp.exp(score - jnp.max(score, -1, keepdims=True))
-        total = jnp.sum(probs, -1, keepdims=True)
-        mixed = mm(probs.astype(BF16), v2[i]) / total
+        inverse = 1.0 / jnp.sum(probs, -1, keepdims=True)
+        mixed = mm(probs.astype(BF16), v2[i]) * inverse
         acc = mixed[:many]
         for h in range(1, HEADS):
             acc = jnp.where(cm[h], mixed[h * many : (h + 1) * many], acc)
-        acc = acc * g2[i]
-        for e in range(halves):
-            af[e, pl.ds(pl.multiple_of(i * many, many), many), :] = acc[:, e * half : (e + 1) * half]
+        return acc * g2[i]
+
+    def column_pair(u, carry):
+        one, two = column(2 * u), column(2 * u + 1)
+        for p in range(n_seq):
+            rng = slice(p * entries, (p + 1) * entries)
+            a2s[p, u] = jnp.concatenate([one[rng], two[rng]], 0).astype(BF16)
+        for t in range(1, n_seq):
+            to = lax.rem(me + t, n_seq)
+            pltpu.make_async_remote_copy(
+                src_ref=a2s.at[to, u],
+                dst_ref=a2r.at[me, u],
+                send_sem=r_send.at[t],
+                recv_sem=r_recv.at[me],
+                device_id={"seq": to},
+                device_id_type=MESH,
+            ).start()
         return carry
 
-    lax.fori_loop(0, ni, column, 0)
-
-    for s in range(many):
-        x = jnp.concatenate(
-            [af[e, pl.ds(s, ni, stride=many), :] for e in range(halves)], 1
-        )
-        a2s[s // entries, s % entries] = x.astype(BF16)
-
-    for t in range(1, n_seq):
-        to = lax.rem(me + t, n_seq)
-        pltpu.make_async_remote_copy(
-            src_ref=a2s.at[to],
-            dst_ref=a2r.at[me],
-            send_sem=r_send.at[t],
-            recv_sem=r_recv.at[me],
-            device_id={"seq": to},
-            device_id_type=MESH,
-        ).start()
+    lax.fori_loop(0, ni // 2, column_pair, 0)
+
     a2r[me] = a2s[me]
     for t in range(1, n_seq):
         whole_copy(t, a2s, a2r, r_send, r_recv).wait_recv()
 
     pair = 2
+    size = pair * ni * entries
     for c in range(0, n_seq, pair):
-        a2 = a2r[c : c + pair].astype(F32).reshape(pair * entries * ni, depth).astype(BF16)
-        m2 = m1b[c : c + pair].reshape(pair * entries * ni, depth) + mm(a2, co[...])
+        rng = slice(c * ni * entries, c * ni * entries + size)
+        a2 = a2r[c : c + pair].reshape(size, depth)
+        m1 = jnp.concatenate([m1b[e, rng, :] for e in range(halves)], 1)
+        m2 = m1 + mm(a2, co[...])
         x3 = norm(m2).astype(BF16)
         hid = jnp.maximum(mm(x3, wide[...]), 0.0).astype(BF16)
-        res = (m2 + mm(hid, narrow[...])).reshape(pair, entries, ni, depth)
-        for e in range(pair):
-            out[:, (c + e) * ni : (c + e + 1) * ni, :] = res[e].astype(BF16)
-
-    for g in (gp, gr, gc, gb):
+        res = m2 + mm(hid, narrow[...])
+        for e in range(halves):
+            m1b[e, rng, :] = res[:, e * half : (e + 1) * half]
+        for s in range(entries):
+            for e in range(halves):
+                out[s, c * ni : (c + pair) * ni, e * half : (e + 1) * half] = m1b[
+                    e, pl.ds(c * ni * entries + s, pair * ni, stride=entries), :
+                ].astype(BF16)
+
+    for g in [gp, gr, gc] + gbs:
         g.drain()
     for t in range(1, n_seq):
         whole_copy(t, x2s, x2t, f_send, f_recv).wait_send()
@@ -382,14 +416,14 @@
         vm((n_res, entries, groups), F32),
         vm((n_seq, entries, groups), F32),
         vm((groups, many), F32),
-        vm((HEADS * rows, 128), F32),
-        vm((n_seq, HEADS * rows, 128), BF16),
+        vm((HEADS * rows // CHUNKS, 128), F32),
+        vm((CHUNKS, n_seq, HEADS * rows // CHUNKS, 128), BF16),
         vm((HEADS, groups, total) if parts == 2 else (1, 16, 128), BF16),
         vm((entries, groups, depth), BF16),
         vm((entries, groups, depth), F32),
         vm((entries, total, depth), BF16),
         vm((entries, total, depth), BF16),
-        vm((n_seq, entries, ni, depth), F32),
+        vm((depth // 128, groups * entries, 128), F32),
         vm((n_seq, entries, ni, depth), BF16),
         vm((n_seq, entries, ni, depth), BF16),
         vm((depth // 128, many * ni, 128), F32),
@@ -397,18 +431,17 @@
         vm((ni, many, depth), BF16),
         vm((ni, many, depth), BF16),
         vm((ni, many, depth), F32),
-        vm((depth // 128, many * ni, 128), F32),
-        vm((n_seq, entries, ni, depth), BF16),
-        vm((n_seq, entries, ni, depth), BF16),
+        vm((n_seq, ni // 2, 2 * entries, depth), BF16),
+        vm((n_seq, ni // 2, 2 * entries, depth), BF16),
     ]
-    for n in (n_res, n_res, n_seq, n_seq, n_seq, n_seq):
-        scratch += [dma((n,)), dma((n,))]
+    for n in ((n_res,), (n_res,), (n_seq,), (CHUNKS, n_seq), (n_seq,), (n_seq,)):
+        scratch += [dma(n), dma(n)]
     operands = (
         hp,
         cp.reshape(parts, rows, jb, cp.shape[-1]),
         present,
         resolved.reshape(1, groups),
-        jnp.pad(wz.T, ((0, 8), (0, 0))),
+        wz,
         *weights,
     )
     spec = pl.BlockSpec(memory_space=pltpu.VMEM)

time: 88.3 us -> 68.8 us (0.78)
  Pallas kernels: 84.9 us -> 65.4 us
    pallas_call x1, Pallas kernels: 84.9 us -> 65.4 us  [on_device(): pl.pallas_call(functools.partial(kernel, n_seq, n_res), out_shape=jax.Sha...]
    unnamed x1 -> x2, local copies, waits for them, and re-layouts: 1.87 us -> 3.27 us
    pad x1 -> x0, local copies, waits for them, and re-layouts: 1.28 us -> none  [on_device(): jnp.pad(wz.T, ((0, 8), (0, 0)))]
where the time goes in v2:
time: 68.8 us; the launch traced here: 68.7 us
  Pallas kernels  65.4 us (95%)
  local copies, waits for them, and re-layouts  3.27 us (5%)
    pallas_call x1, Pallas kernels, on_device(): pl.pallas_call(functools.partial(kernel, n_seq, n_res), out_shape=jax.Sha...  65.4 us
    unnamed x2, local copies, waits for them, and re-layouts  3.27 us

profile of v2, /device:TPU:0, one launch (start us, length us, event | category | flops | bytes accessed | tf_op | source)
XLA Modules:
  0.0 68.7 jit_solution(11351055952986563324)
XLA Ops:
  0.0 1.4 %copy.18.wz = bf16[128,8]{1,0:T(8,128)(2,1)} copy(bf16[128,8]{0,1:T(8,128)(2,1)} %param.21) | data formatting | bytes 4096 | tf_op args[4]
  1.4 65.4 %shard_map.163 = bf16[8,128,256]{2,1,0:T(8,128)(2,1)} custom-call(bf16[8,128,256]{2,1,0:T(8,128)(2,1)} %hp.1, bf16[2,64,64,128]{3,2,1,0:T(8,128)(2,1)} %bitcast.2, s32[8,128]{1,0:T(8,128)} %present.1, s32[1,128]{1,0:T(1,128)} %bitcast.3, bf16[128,8]{1,0:T(8,128)(2,1)} %copy.18.wz, bf16[256,256]{1,0:T(8,128)(2,1)} %wq.1, bf16[256,256]{1,0:T(8,128)(2,1)} %wk.1, ...), custom_call_target="tpu_custom_call" | custom-call | tf_op jit(solution)/shard_map/pallas_call | solution.py:448
  66.8 1.9 %copy.20 = bf16[8,128,256]{2,1,0:T(8,128)(2,1)} copy(bf16[8,128,256]{2,1,0:T(8,128)(2,1)} %shard_map.163) | data formatting | bytes 1048576

commit v3 on v2

--- a/solution.py
+++ b/solution.py
@@ -11,8 +11,10 @@
 HEAD_DIM = 32
 EPS = 1e-05
 MASK_SCALE = 1000000000.0
-CHUNKS = 2
+CHUNKS = 4
 TOGETHER = 4
+SEQS = 4
+COLS = 4
 MESH = pl.DeviceIdType.MESH
 BF16 = jnp.bfloat16
 F32 = jnp.float32
@@ -171,7 +173,7 @@
 
     step = 8
     some = rows // CHUNKS
-    wzt = jnp.transpose(wz[...].astype(F32)).astype(BF16)
+    wzt = wz[...]
 
     def bias_block(a, b, carry):
         wide_rows = cp[:, pl.ds(a * some + b * step, step)].astype(F32)
@@ -191,33 +193,37 @@
         brecv[a, me] = bstage[...].astype(BF16)
         gbs[a].start()
 
-    def own_side(s, carry):
-        x = norm(hp[s].astype(F32)).astype(BF16)
-        q1[s] = (mm(x, wq[...]) * scale).astype(BF16)
-        g1[s] = jax.nn.sigmoid(mm(x, wg[...]))
+    def own_side(u, carry):
+        rng = pl.ds(u * SEQS, SEQS)
+        x = norm(hp[rng].astype(F32).reshape(SEQS * groups, depth)).astype(BF16)
+        q1[rng] = (mm(x, wq[...]) * scale).astype(BF16).reshape(SEQS, groups, depth)
+        g1[rng] = jax.nn.sigmoid(mm(x, wg[...])).reshape(SEQS, groups, depth)
         return carry
 
-    lax.fori_loop(0, entries, own_side, 0)
+    lax.fori_loop(0, entries // SEQS, own_side, 0)
 
     def key_side(r):
-        start = pl.multiple_of(r * groups, groups)
-
-        def one(s, carry):
-            x = norm(prof[r, s].astype(F32)).astype(BF16)
-            k1[s, pl.ds(start, groups), :] = mm(x, wk[...]).astype(BF16)
-            v1[s, pl.ds(start, groups), :] = mm(x, wv[...]).astype(BF16)
+        keys = pl.ds(pl.multiple_of(r * groups, groups), groups)
+
+        def some_seqs(u, carry):
+            rng = pl.ds(u * SEQS, SEQS)
+            x = norm(prof[r, rng].astype(F32).reshape(SEQS * groups, depth)).astype(BF16)
+            k1[rng, keys, :] = mm(x, wk[...]).astype(BF16).reshape(SEQS, groups, depth)
+            v1[rng, keys, :] = mm(x, wv[...]).astype(BF16).reshape(SEQS, groups, depth)
             return carry
 
-        lax.fori_loop(0, entries, one, 0)
+        lax.fori_loop(0, entries // SEQS, some_seqs, 0)
 
     key_side(mine)
-    for t in range(1, gbs[0].far + 1):
-        gbs[0].forward(t)
+    for gb in gbs[: CHUNKS // 2]:
+        for t in range(1, gb.far + 1):
+            gb.forward(t)
     for t in range(1, gp.far + 1):
         gr.forward(t)
         gp.forward(t)
-    for t in range(1, gbs[1].far + 1):
-        gbs[1].forward(t)
+    for gb in gbs[CHUNKS // 2 :]:
+        for t in range(1, gb.far + 1):
+            gb.forward(t)
     for t in range(1, gc.far + 1):
         gc.forward(t)
     for t in range(1, gp.far + 1):
@@ -227,18 +233,17 @@
         gr.finish(t)
     for t in range(0, gc.far + 1):
         gc.finish(t)
-    for gb in gbs:
+
+    cmask_t[...] = jnp.transpose(cmask[...].reshape(many, groups))
+
+    first = lax.broadcasted_iota(jnp.int32, (some, 2 * jb), 1) < jb
+    for a, gb in enumerate(gbs):
         for t in range(0, gb.far + 1):
             gb.finish(t)
-
-    cmask_t[...] = jnp.transpose(cmask[...].reshape(many, groups))
-
-    if parts == 2:
-        first = lax.broadcasted_iota(jnp.int32, (some, 2 * jb), 1) < jb
-        for h in range(HEADS):
-            for c in range(n_seq // 2):
-                cols = slice(c * 2 * jb, (c + 1) * 2 * jb)
-                for a in range(CHUNKS):
+        if parts == 2:
+            for h in range(HEADS):
+                for c in range(n_seq // 2):
+                    cols = slice(c * 2 * jb, (c + 1) * 2 * jb)
                     left = brecv[a, 2 * c, h * some : (h + 1) * some, :].astype(F32)
                     right = brecv[a, 2 * c + 1, h * some : (h + 1) * some, :].astype(F32)
                     top = jnp.where(first, left, pltpu.roll(right, jb, 1))
@@ -261,7 +266,7 @@
 
     hmask = [head_mask(groups, depth, h) for h in range(HEADS)]
 
-    def row(s, carry):
+    def row(s):
         q = q1[s]
         kk = k1[s]
         vv = v1[s]
@@ -286,16 +291,21 @@
                 )
         a1 = (acc * g1[s]).astype(BF16)
         m1 = hp[s].astype(F32) + mm(a1, wo[...])
-        x2 = norm(m1)
-        for e in range(halves):
-            m1b[e, pl.ds(s, groups, stride=entries), :] = m1[:, e * half : (e + 1) * half]
-        for p in range(n_seq):
-            x2s[p, s] = x2[p * ni : (p + 1) * ni].astype(BF16)
+        return m1, norm(m1)
+
+    def row_pair(u, carry):
+        results = [row(2 * u), row(2 * u + 1)]
+        for z, (m1, x2) in enumerate(results):
+            s = 2 * u + z
+            for e in range(halves):
+                m1b[e, pl.ds(s, groups, stride=entries), :] = m1[:, e * half : (e + 1) * half]
+            for p in range(n_seq):
+                x2s[p, s] = x2[p * ni : (p + 1) * ni].astype(BF16)
         for t in range(1, n_seq):
             to = lax.rem(me + t, n_seq)
             pltpu.make_async_remote_copy(
-                src_ref=x2s.at[to, s],
-                dst_ref=x2t.at[me, s],
+                src_ref=x2s.at[to, pl.ds(2 * u, 2)],
+                dst_ref=x2t.at[me, pl.ds(2 * u, 2)],
                 send_sem=f_send.at[t],
                 recv_sem=f_recv.at[me],
                 device_id={"seq": to},
@@ -303,7 +313,7 @@
             ).start()
         return carry
 
-    lax.fori_loop(0, entries, row, 0)
+    lax.fori_loop(0, entries // 2, row_pair, 0)
 
     def whole_copy(t, src, dst, send, recv):
         origin = lax.rem(me + n_seq - t, n_seq)
@@ -353,16 +363,21 @@
             acc = jnp.where(cm[h], mixed[h * many : (h + 1) * many], acc)
         return acc * g2[i]
 
-    def column_pair(u, carry):
-        one, two = column(2 * u), column(2 * u + 1)
+    pairs = COLS // 2
+
+    def column_group(u, carry):
+        done = [column(COLS * u + z) for z in range(COLS)]
         for p in range(n_seq):
             rng = slice(p * entries, (p + 1) * entries)
-            a2s[p, u] = jnp.concatenate([one[rng], two[rng]], 0).astype(BF16)
+            for z in range(pairs):
+                a2s[p, pairs * u + z] = jnp.concatenate(
+                    [done[2 * z][rng], done[2 * z + 1][rng]], 0
+                ).astype(BF16)
         for t in range(1, n_seq):
             to = lax.rem(me + t, n_seq)
             pltpu.make_async_remote_copy(
-                src_ref=a2s.at[to, u],
-                dst_ref=a2r.at[me, u],
+                src_ref=a2s.at[to, pl.ds(pairs * u, pairs)],
+                dst_ref=a2r.at[me, pl.ds(pairs * u, pairs)],
                 send_sem=r_send.at[t],
                 recv_sem=r_recv.at[me],
                 device_id={"seq": to},
@@ -370,13 +385,13 @@
             ).start()
         return carry
 
-    lax.fori_loop(0, ni // 2, column_pair, 0)
+    lax.fori_loop(0, ni // COLS, column_group, 0)
 
     a2r[me] = a2s[me]
     for t in range(1, n_seq):
         whole_copy(t, a2s, a2r, r_send, r_recv).wait_recv()
 
-    pair = 2
+    pair = 4
     size = pair * ni * entries
     for c in range(0, n_seq, pair):
         rng = slice(c * ni * entries, c * ni * entries + size)
@@ -441,7 +456,7 @@
         cp.reshape(parts, rows, jb, cp.shape[-1]),
         present,
         resolved.reshape(1, groups),
-        wz,
+        wz.T,
         *weights,
     )
     spec = pl.BlockSpec(memory_space=pltpu.VMEM)

time: 68.8 us -> 62.7 us (0.911)
  Pallas kernels: 65.4 us -> 60.6 us
  local copies, waits for them, and re-layouts: 3.27 us -> 1.87 us
    pallas_call x1, Pallas kernels: 65.4 us -> 60.6 us  [on_device(): pl.pallas_call(functools.partial(kernel, n_seq, n_res), out_shape=jax.Sha...]
    unnamed x2 -> x1, local copies, waits for them, and re-layouts: 3.27 us -> 1.87 us
where the time goes in v3:
time: 62.7 us; the launch traced here: 62.5 us
  Pallas kernels  60.6 us (97%)
  local copies, waits for them, and re-layouts  1.87 us (3%)
    pallas_call x1, Pallas kernels, on_device(): pl.pallas_call(functools.partial(kernel, n_seq, n_res), out_shape=jax.Sha...  60.6 us
    unnamed x1, local copies, waits for them, and re-layouts  1.87 us

profile of v3, /device:TPU:0, one launch (start us, length us, event | category | flops | bytes accessed | tf_op | source)
XLA Modules:
  0.0 62.5 jit_solution(4468351538385323397)
XLA Ops:
  0.0 60.6 %shard_map.163 = bf16[8,128,256]{2,1,0:T(8,128)(2,1)} custom-call(bf16[8,128,256]{2,1,0:T(8,128)(2,1)} %hp.1, bf16[2,64,64,128]{3,2,1,0:T(8,128)(2,1)} %bitcast.3, s32[8,128]{1,0:T(8,128)} %present.1, s32[1,128]{1,0:T(1,128)} %bitcast.5, bf16[8,128]{1,0:T(8,128)(2,1)} %bitcast.4, bf16[256,256]{1,0:T(8,128)(2,1)} %wq.1, bf16[256,256]{1,0:T(8,128)(2,1)} %wk.1, ...), custom_call_target="tpu_custom_call" | custom-call | tf_op jit(solution)/shard_map/pallas_call | solution.py:463
  60.6 1.9 %copy.19 = bf16[8,128,256]{2,1,0:T(8,128)(2,1)} copy(bf16[8,128,256]{2,1,0:T(8,128)(2,1)} %shard_map.163) | data formatting | bytes 1048576
